TPU v7x, 128 devices: a whole 4x4x4 slice. The times are simulated.
128 devices in a mesh: chan: 8 (over x, y_lo), panel: 16 (over z, y_hi, core).
Axes of the slice: x: 4, y: 4 (y_hi: 2, y_lo: 2; y = y_hi * 2 + y_lo), z: 4, core: 2. Of those that a mesh axis runs over, the one named last changes fastest.
Arguments:
- voltages: bfloat16 [2048, 536576], P(('chan', 'panel')), may hold values from -6 to 6
- prototype: float32 [4, 4096], replicated, may hold values from -0.046875 to 0.046875
- complex_gains: float32 [2048, 96], P(('chan', 'panel')), may hold values from -4 to 4
- flagged: int32 [1024], P(('chan', 'panel')), may hold values 0 or 1
- station_order: int32 [1024], replicated, may hold values from 0 to 1023, each once
Outputs:
- visibilities: bfloat16 [2, 48, 2048, 2048], P(None, 'chan', 'panel')
Inputs may be any that keep to these rules, and one draw needn't show every extreme that they name: `station_order`: each station appears once.
All inputs are finite; a program needn't handle non-finite values. No bound on the sum of `flagged` on one device may be relied on, other than what follows from the above.
Results may differ from a plain program's by a relative error of at most 0.0073.
Values may be sent and summed in bfloat16 or wider, within the bound.
A program may use at most 128 MiB of HBM per device.

v0:
```python
import math

import jax
import jax.numpy as jnp
from jax import lax
from jax.sharding import PartitionSpec as P


def make_table(length, channels):
    sample = jnp.arange(length, dtype=jnp.int32)[:, None]
    column = length // 4 + jnp.arange(channels, dtype=jnp.int32)[None, :]
    phases = (sample * column % length).astype(jnp.float32) * (2.0 * math.pi / length)
    stacked = jnp.stack([jnp.cos(phases), -jnp.sin(phases)], axis=2)
    return stacked.reshape(length, 2 * channels).astype(jnp.bfloat16)


def windowed(shaped_volt, prototype, first_frame, count):
    accumulated = jnp.zeros((shaped_volt.shape[0], count, shaped_volt.shape[2]), jnp.float32)
    for tap_index in range(prototype.shape[0]):
        start = first_frame + tap_index
        accumulated = accumulated + prototype[tap_index][None, None, :] * shaped_volt[
            :, start : start + count, :
        ].astype(jnp.float32)
    return accumulated.astype(jnp.bfloat16)


def spectra_of(shaped_volt, prototype, dft_table, complex_gains, keeping, first_frame, count):
    frames_win = windowed(shaped_volt, prototype, first_frame, count)
    raw_spectra = jnp.einsum(
        "nk,ifn->kif", dft_table, frames_win, preferred_element_type=jnp.float32
    )
    channels = dft_table.shape[1] // 2
    local_inputs = shaped_volt.shape[0]
    shaped = raw_spectra.reshape(channels, 2, local_inputs, count)
    gain_parts = complex_gains.T.reshape(channels, 2, local_inputs)[:, :, :, None]
    real_part = gain_parts[:, 0] * shaped[:, 0] - gain_parts[:, 1] * shaped[:, 1]
    imag_part = gain_parts[:, 0] * shaped[:, 1] + gain_parts[:, 1] * shaped[:, 0]
    stacked = jnp.stack([real_part, imag_part], axis=2) * keeping[None, :, None, None]
    return stacked.reshape(channels, local_inputs, 2 * count).astype(jnp.bfloat16)


def local(voltages, prototype, complex_gains, flagged, station_order):
    local_inputs = voltages.shape[0]
    length = prototype.shape[1]
    tap_count = prototype.shape[0]
    channels = complex_gains.shape[1] // 2
    frame_total = voltages.shape[1] // length - tap_count + 1
    shaped_volt = voltages.reshape(local_inputs, frame_total + tap_count - 1, length)
    keeping = jnp.repeat(1.0 - flagged.astype(jnp.float32), 2)
    dft_table = make_table(length, channels)
    chan_size = lax.axis_size("chan")
    panel_size = lax.axis_size("panel")
    inputs_all = 2 * station_order.shape[0]
    panel_width = inputs_all // panel_size
    position = jnp.arange(inputs_all, dtype=jnp.int32)
    source = 2 * station_order[position // 2] + position % 2
    device_of = source // local_inputs
    within = source % local_inputs
    local_row = (
        device_of % panel_size * (chan_size * local_inputs)
        + device_of // panel_size * local_inputs
        + within
    )
    mine = lax.dynamic_slice_in_dim(local_row, lax.axis_index("panel") * panel_width, panel_width)
    spectra = spectra_of(shaped_volt, prototype, dft_table, complex_gains, keeping, 0, frame_total)
    turned = lax.all_to_all(spectra, "chan", split_axis=0, concat_axis=1, tiled=True)
    gathered = lax.all_gather(turned, "panel", axis=1, tiled=True)
    columns = jnp.take(gathered, local_row, axis=1)
    picked = jnp.take(gathered, mine, axis=1)
    count = picked.shape[2] // 2
    swapped = jnp.concatenate([picked[:, :, count:], -picked[:, :, :count]], axis=2)
    left = jnp.stack([picked, swapped], axis=1)
    accumulated = jnp.einsum("cspt,cqt->scpq", left, columns, preferred_element_type=jnp.float32)
    return (accumulated * (1.0 / frame_total)).astype(jnp.bfloat16)


def solution(mesh):
    placed = (
        P(("chan", "panel"), None),
        P(),
        P(("chan", "panel"), None),
        P(("chan", "panel")),
        P(),
    )
    return jax.shard_map(
        local, mesh=mesh, in_specs=placed, out_specs=P(None, "chan", "panel", None), check_vma=False
    )
```

profile of v0, /device:TPU:1, one launch (start us, length us, event | category | flops | bytes accessed | tf_op | source)
XLA Modules:
  0.0 216.5 jit_solution(17362298748870532838)
XLA Ops:
  6.5 1.1 fusion.40
  7.6 3.7 %cosine_convert_fusion = (bf16[4096,48,1]{0,1,2:T(8,128)(2,1)S(1)}, bf16[4096,48,1]{0,1,2:T(8,128)(2,1)S(1)}) fusion(s32[48]{0:T(128)S(1)} %iota_add_fusion), kind=kLoop, calls=%fused_computation.25 | loop fusion | flops 3342336 | bytes 786624 | tf_op jit(solution)/shard_map/convert
  11.4 0.8 copy.35
  12.2 0.3 convert_element_type.48
  12.5 0.5 dot_general.11
  13.0 21.9 %reshape.405 = bf16[16,131,4096]{2,1,0:T(8,128)(2,1)} reshape(bf16[16,536576]{1,0:T(8,128)(2,1)} %param.5) | data formatting | bytes 34340864 | tf_op jit(solution)/shard_map/reshape | solution.py:48
  35.2 37.8 %fusion.1 = f32[48,2,16,128]{3,0,2,1:T(8,128)S(1)} fusion(bf16[16,131,4096]{2,1,0:T(8,128)(2,1)} %reshape.405, f32[4096]{0:T(1024)S(1)} %bitcast.63, f32[4096]{0:T(1024)S(1)} %bitcast.64, f32[4096]{0:T(1024)S(1)} %bitcast.62, f32[4096]{0:T(1024)S(1)} %bitcast.61, bf16[48,2,4096,1]{2,1,0,3:T(2,128)(2,1)S(1)} %bitcast.54), kind=kOutput, calls=%fused_computation.5 | convolution fusion | flops 1711276032 | bytes 68747264 | tf_op jit(solution)/shard_map/nk,ifn->kif/dot_general | solution.py:29
  73.0 0.3 multiply_subtract_fusion
  73.3 0.6 copy.38
  73.9 0.6 stack.22
  74.7 0.1 multiply_convert_fusion.1
  74.9 12.8 %all_to_all.18 = bf16[48,16,256]{2,1,0:T(8,128)(2,1)S(1)} all-to-all(bf16[48,16,256]{2,1,0:T(8,128)(2,1)S(1)} %multiply_convert_fusion.1), channel_id=1, replica_groups=mesh['chan'=8,'panel'=16] {'chan'}, dimensions={0} | all-to-all | bytes 786432 | tf_op jit(solution)/shard_map/all_to_all | solution.py:66
  87.7 0.8 copy.39
  88.6 8.6 %gather_fusion = s32[2048]{0:T(1024)S(1)} fusion(s32[1024]{0:T(1024)S(1)} %copy-done, s32[2048]{0:T(1024)S(1)} %broadcast_clamp_fusion.1), kind=kCustom, calls=%fused_computation | custom fusion | bytes 24576 | tf_op jit(solution)/shard_map/gather | solution.py:56
  97.3 0.1 compare_select_fusion
  97.4 58.1 %all-gather.2.cloned.1.call-done = bf16[6,2048,256]{2,1,0:T(8,128)(2,1)} async-done(((bf16[6,128,256]{2,1,0:T(8,128)(2,1)}), bf16[6,2048,256]{2,1,0:T(8,128)(2,1)}) %all-gather.2.cloned.1.call-update) | async-done | bytes 6291472 | tf_op jit(solution)/shard_map/all_gather | solution.py:67
  155.5 8.8 %copy.40 = bf16[6,2048,256]{2,0,1:T(8,128)(2,1)} copy(bf16[6,2048,256]{2,1,0:T(8,128)(2,1)} %all-gather.2.cloned.1.call-done) | data formatting | bytes 12582912 | tf_op jit(solution)/shard_map/all_gather | solution.py:67
  164.4 4.0 %gather_fusion.2 = bf16[128,6,256]{2,1,0:T(8,128)(2,1)S(1)} fusion(bf16[6,2048,256]{2,0,1:T(8,128)(2,1)} %copy.40, s32[1024]{0:T(1024)S(1)} %pad_clamp_fusion), kind=kCustom, calls=%fused_computation.2 | custom fusion | bytes 786944 | tf_op jit(solution)/shard_map/jit(_take)/gather | solution.py:69
  168.4 0.1 bitcast_select_fusion.1
  168.5 0.1 fusion.18
  168.7 19.2 %gather_fusion.1 = bf16[2048,6,256]{2,1,0:T(8,128)(2,1)} fusion(bf16[6,2048,256]{2,0,1:T(8,128)(2,1)} %copy.40, s32[2048]{0:T(1024)S(1)} %broadcast_clamp_fusion), kind=kCustom, calls=%fused_computation.1 | custom fusion | bytes 12591104 | tf_op jit(solution)/shard_map/jit(_take)/gather | solution.py:68
  188.0 8.5 %select_bitcast_fusion = bf16[6,2048,256,1]{2,0,1,3:T(8,128)(2,1)S(1)} fusion(bf16[2048,6,256]{2,1,0:T(8,128)(2,1)} %gather_fusion.1, pred[2048]{0:T(1024)(128)(4,1)S(1)} %get-tuple-element.7), kind=kLoop, calls=%fused_computation.7 | loop fusion | flops 3145728 | bytes 12584960 | tf_op jit(solution)/shard_map/jit(_take)/select_n | solution.py:68
  196.5 4.6 %fusion.3 = bf16[2,6,128,2048]{2,3,0,1:T(8,128)(2,1)} fusion(bf16[6,2048,256,1]{2,0,1,3:T(8,128)(2,1)S(1)} %select_bitcast_fusion, bf16[6,1,128,256]{3,2,1,0:T(8,128)(2,1)S(1)} %maximum_bitcast_fusion, bf16[6,1,128,256]{3,2,1,0:T(8,128)(2,1)S(1)} %fusion.18), kind=kOutput, calls=%fused_computation.8 | convolution fusion | flops 1618477056 | bytes 13369344 | tf_op jit(solution)/shard_map/cspt,cqt->scpq/dot_general | solution.py:73
  201.1 8.6 %copy.45 = bf16[2,6,128,2048]{3,2,1,0:T(8,128)(2,1)} copy(bf16[2,6,128,2048]{2,3,0,1:T(8,128)(2,1)} %fusion.3) | data formatting | bytes 12582912 | tf_op jit(solution)/shard_map/convert_element_type | solution.py:74
  (27 shorter events, 0.8 us)
Async XLA Ops:
  6.5 82.0 %copy-start = (s32[1024]{0:T(1024)S(1)}, s32[1024]{0:T(1024)}, u32[]{:S(2)}) copy-start(s32[1024]{0:T(1024)} %param.9) | copy-start | bytes 12292
  6.5 149.0 %all-gather.2.cloned.1.call-start = ((), (), s32[]{:S(2)}) async-start(), calls=%async_computation.1 | async-start | bytes 6684672 | tf_op jit(solution)/shard_map/all_gather | solution.py:67
  13.0 21.9 %copy-start.1 = (f32[16,96]{1,0:T(8,128)S(1)}, f32[16,96]{1,0:T(8,128)}, u32[]{:S(2)}) copy-start(f32[16,96]{1,0:T(8,128)} %param.7) | copy-start | bytes 18436
  35.2 39.4 %copy-start.2 = (s32[8]{0:T(128)S(1)}, s32[8]{0:T(128)}, u32[]{:S(2)}) copy-start(s32[8]{0:T(128)} %param.8) | copy-start | bytes 100
Sparse Core Ops, SparseCore 0:
  88.6 66.8 all-gather.1
where the time goes:
time: 217 us
  local copies, waits for them, and re-layouts  76.3 us (35%)
  waiting for transfers between devices  58.1 us (27%)
  matrix products  42.3 us (19%)
  between operations  13.6 us (6%)
  other arithmetic  13.4 us (6%)
  blocking collectives  12.8 us (6%)
    all_gather x1, waiting for transfers between devices, local(): gathered = lax.all_gather(turned, 'panel', axis=1, tiled=True)  58.1 us
    dot_general x1, matrix products, spectra_of(): jnp.einsum('nk,ifn->kif', dft_table, frames_win, preferred_element_type=j...  37.8 us
    reshape x1, local copies, waits for them, and re-layouts, local(): voltages.reshape(local_inputs, frame_total + tap_count - 1, length)  21.9 us
    gather x1, local copies, waits for them, and re-layouts, local(): columns = jnp.take(gathered, local_row, axis=1)  19.2 us
    all_to_all x1, blocking collectives, local(): lax.all_to_all(spectra, 'chan', split_axis=0, concat_axis=1, tiled=True)  12.8 us
    all_gather x1, local copies, waits for them, and re-layouts, local(): gathered = lax.all_gather(turned, 'panel', axis=1, tiled=True)  8.84 us
    select_n x2, other arithmetic, local(): columns = jnp.take(gathered, local_row, axis=1)  8.68 us
    convert_element_type x1, local copies, waits for them, and re-layouts, local(): return (accumulated * (1.0 / frame_total)).astype(jnp.bfloat16)  8.63 us
  transfers between devices with their start and end apart: 1, of which 1 were waited for; matrix products, arithmetic and copies ran while one was open for 4% of the time, Pallas kernels for 0%

commit v1 on v0

v1 whole, which is shorter than its diff:
```python
import functools
import math

import jax
import jax.numpy as jnp
import numpy as np
from jax import lax
from jax.experimental import pallas as pl
from jax.experimental.pallas import tpu as pltpu
from jax.sharding import PartitionSpec as P

MESH = pl.DeviceIdType.MESH
F32, BF16 = jnp.float32, jnp.bfloat16
NT = (((1,), (1,)), ((), ()))

NFFT, TAPS, FRAMES, NCHAN = 4096, 4, 128, 48
INPUTS, STATIONS = 2048, 1024
LOCAL = 16
GROUPS, PER = 8, 6
FALL = FRAMES + TAPS - 1
PIECE = LOCAL * 2 * PER
BLOCK = GROUPS * PIECE
PANELS = 16
CHUNK_F = 33
STARTS = (0, 33, 66, 98)


def table_rows():
    n = np.arange(NFFT)[None, :]
    j = np.arange(NCHAN)[:, None]
    m = (n * (NFFT // 4 + j)) % NFFT
    phase = m.astype(np.float32) * np.float32(2.0 * math.pi / NFFT)
    both = np.stack([np.cos(phase), -np.sin(phase)], axis=1)
    both = both.reshape(GROUPS, PER, 2, NFFT).transpose(0, 2, 1, 3)
    both = np.pad(both, ((0, 0), (0, 0), (0, 8 - PER), (0, 0)))
    return both.reshape(128, NFFT).astype(jnp.bfloat16)


def channelize_kernel(volt, proto, table, gre, gim, out, buf, w, y, s, sems):
    def load(q):
        cols = pl.ds((STARTS[q] if q < 3 else 99) * NFFT, (33 if q < 3 else 32) * NFFT)
        return pltpu.make_async_copy(volt.at[:, cols], buf.at[:, cols], sems.at[q])

    for q in range(4):
        load(q).start()

    tab = 512

    def weights(i, _):
        cols = pl.ds(pl.multiple_of(i * tab, tab), tab)
        t = table[:, cols].astype(F32)
        for tap in range(TAPS):
            w[pl.ds(tap * 128, 128), cols] = (t * proto[tap : tap + 1, cols]).astype(BF16)
        return 0

    lax.fori_loop(0, NFFT // tab, weights, 0)

    kw = 1024
    for q in range(4):
        load(q).wait()
        first = STARTS[q]
        rows = pl.ds(first * LOCAL, CHUNK_F * LOCAL)

        def step(i, _):
            k = pl.multiple_of(i * kw, kw)
            x = jnp.concatenate([buf[:, pl.ds(k + (first + f) * NFFT, kw)] for f in range(CHUNK_F)], axis=0)
            for h in range(2):
                prod = lax.dot_general(x, w[pl.ds(h * 256, 256), pl.ds(k, kw)], NT, preferred_element_type=F32)
                for u in range(2):
                    part = prod[:, u * 128 : u * 128 + 128]
                    t = 2 * h + u

                    @pl.when(i == 0)
                    def _():
                        y[t, rows, :] = part

                    @pl.when(i > 0)
                    def _():
                        y[t, rows, :] += part
            return 0

        lax.fori_loop(0, NFFT // kw, step, 0)

    for i in range(LOCAL):
        raw = y[0, pl.ds(i, FRAMES, stride=LOCAL), :]
        for t in range(1, TAPS):
            raw = raw + y[t, pl.ds(t * LOCAL + i, FRAMES, stride=LOCAL), :]
        turned = raw.T
        for g in range(GROUPS):
            re, im = turned[g * 16 : g * 16 + 8], turned[g * 16 + 8 : g * 16 + 16]
            a, b = gre[g * 8 : g * 8 + 8, i : i + 1], gim[g * 8 : g * 8 + 8, i : i + 1]
            at = g * PIECE + i * 2 * PER
            s[at : at + PER, :] = (a * re - b * im)[:PER]
            s[at + PER : at + 2 * PER, :] = (a * im + b * re)[:PER]
    out[...] = s[...].astype(BF16)


def channelize(volt, proto, gre, gim):
    vm = pl.BlockSpec(memory_space=pltpu.VMEM)
    return pl.pallas_call(
        channelize_kernel,
        out_shape=jax.ShapeDtypeStruct((BLOCK, 128), BF16),
        in_specs=[pl.BlockSpec(memory_space=pl.ANY), vm, vm, vm, vm],
        out_specs=vm,
        scratch_shapes=[
            pltpu.VMEM((LOCAL, FALL * NFFT), BF16),
            pltpu.VMEM((TAPS * 128, NFFT), BF16),
            pltpu.VMEM((TAPS, FALL * LOCAL, 128), F32),
            pltpu.VMEM((BLOCK, 128), F32),
            pltpu.SemaphoreType.DMA((4,)),
        ],
        compiler_params=pltpu.CompilerParams(vmem_limit_bytes=56 * 2**20),
        cost_estimate=pl.CostEstimate(flops=2 * 2096 * 4096 * 512, bytes_accessed=20 * 2**20, transcendentals=0),
        name="channelize",
    )(volt, proto, jnp.asarray(table_rows()), gre, gim)


CHUNK = BLOCK // 4
HALF = CHUNK // 2
ORDER = (0, 1, 3, 2)
Z_FIRST = (0, 3)


def exchange_kernel(src, out, ss, rs, own_sem):
    c, p = lax.axis_index("chan"), lax.axis_index("panel")
    x, yl = c // 2, c % 2
    z, h, k = p // 4, (p // 2) % 2, p % 2

    def panel(dz, dh, dk=0):
        return ((z + dz) % 4) * 4 + ((h + dh) % 2) * 2 + (k + dk) % 2

    def at_panel(pan):
        return {"chan": c, "panel": pan}

    up, down, over, sib = (at_panel(a) for a in (panel(1, 0), panel(3, 0), panel(0, 1), panel(0, 0, 1)))

    def chan_target(r):
        return ((x + 4 - r // 2) % 4) * 2 + (yl + r % 2) % 2

    barrier = pltpu.get_barrier_semaphore()
    greet = [{"chan": chan_target(r), "panel": p} for r in range(1, 8)] + [up, down, over, sib]
    for d in greet:
        pl.semaphore_signal(barrier, inc=1, device_id=d, device_id_type=MESH)
    pl.semaphore_wait(barrier, len(greet))

    ids, sends = {}, []

    def number(name):
        return ids.setdefault(name, len(ids))

    def region(block, row, rows):
        return out.at[pl.ds(pl.multiple_of(block * BLOCK + row, 16), rows)]

    def send(name, block, row, rows, device, source=None):
        n = number(name)
        there = region(block, row, rows)
        copy = pltpu.make_async_remote_copy(
            there if source is None else source, there, ss.at[n], rs.at[n], device_id=device, device_id_type=MESH
        )
        copy.start()
        sends.append(copy)

    def arrived(name, block, row, rows):
        n = number(name)
        here = region(block, row, rows)
        pltpu.make_async_remote_copy(here, here, ss.at[n], rs.at[n], device_id=sib, device_id_type=MESH).wait_recv()

    shared = []

    def share(block_d, row, rows):
        name = ("s", block_d, row)
        send(name, panel(*block_d), row, rows, sib)
        shared.append((name, block_d, row, rows))

    mine = panel(0, 0)
    own = pltpu.make_async_copy(src.at[pl.ds(pl.multiple_of(c * PIECE, 16), PIECE)], region(mine, 0, PIECE), own_sem)
    own.start()
    for r in (1, 2, 3, 6, 7, 4, 5):
        t = chan_target(r)
        piece = src.at[pl.ds(pl.multiple_of(t * PIECE, 16), PIECE)]
        send(("a", r), mine, r * PIECE, PIECE, {"chan": t, "panel": p}, piece)

    def own_chunk(q):
        for r in (2 * q, 2 * q + 1):
            if r == 0:
                own.wait()
            else:
                arrived(("a", r), mine, r * PIECE, PIECE)
        row = q * CHUNK
        if q not in Z_FIRST:
            send(("y", 0, q), mine, row, CHUNK, over)
        send(("up", 0, q), mine, row, CHUNK, up)
        send(("down", 0, q), mine, row, CHUNK, down)
        if q in Z_FIRST:
            send(("y", 0, q), mine, row, CHUNK, over)
        share((0, 0), row, CHUNK)

    def near(dh, q):
        row = q * CHUNK
        for dz, got, way, half, name in ((3, "up", up, 0, "fup"), (1, "down", down, HALF, "fdown")):
            block = panel(dz, dh)
            arrived((got, dh, q), block, row, CHUNK)
            send((name, dh, q), block, row + half, HALF, way)
            if dh == 0 and q in Z_FIRST:
                send(("y", dz, q), block, row, CHUNK, over)
            share((dz, dh), row, CHUNK)

    def far(dh, q):
        row = q * CHUNK
        block = panel(2, dh)
        for name, half in (("fup", 0), ("fdown", HALF)):
            arrived((name, dh, q), block, row + half, HALF)
            if dh == 0 and q in Z_FIRST:
                send(("y", 2, q, half), block, row + half, HALF, over)
            share((2, dh), row + half, HALF)

    def partner(q):
        row, block = q * CHUNK, panel(0, 1)
        arrived(("y", 0, q), block, row, CHUNK)
        send(("up", 1, q), block, row, CHUNK, up)
        send(("down", 1, q), block, row, CHUNK, down)
        share((0, 1), row, CHUNK)

    def from_over(q):
        row = q * CHUNK
        for dz in (0, 3, 1):
            arrived(("y", dz, q), panel(dz, 1), row, CHUNK)
            share((dz, 1), row, CHUNK)
        for half in (0, HALF):
            arrived(("y", 2, q, half), panel(2, 1), row + half, HALF)
            share((2, 1), row + half, HALF)

    own_chunk(0)
    own_chunk(1)
    near(0, 0)
    own_chunk(3)
    own_chunk(2)
    partner(1)
    near(0, 1)
    far(0, 0)
    near(0, 3)
    partner(2)
    near(0, 2)
    far(0, 1)
    far(0, 3)
    near(1, 1)
    from_over(0)
    far(0, 2)
    near(1, 2)
    far(1, 1)
    from_over(3)
    far(1, 2)

    for name, (dz, dh), row, rows in shared:
        arrived(name, panel(dz, dh, 1), row, rows)
    for copy in sends:
        copy.wait_send()


def exchange(pieces):
    many = 128
    anywhere = pl.BlockSpec(memory_space=pl.ANY)
    return pl.pallas_call(
        exchange_kernel,
        out_shape=jax.ShapeDtypeStruct((PANELS * BLOCK, 128), BF16),
        in_specs=[anywhere],
        out_specs=anywhere,
        scratch_shapes=[
            pltpu.SemaphoreType.DMA((many,)),
            pltpu.SemaphoreType.DMA((many,)),
            pltpu.SemaphoreType.DMA,
        ],
        compiler_params=pltpu.CompilerParams(collective_id=0, has_side_effects=True),
        name="exchange",
    )(pieces)


LOADS = 8
UNIT = 2 * 2 * PER


def correlate_kernel(place, spectra, out, raw, wide, sorted_, ordered, sems):
    ch = pl.program_id(0)

    @pl.when(ch == 0)
    def _():
        part = PANELS * BLOCK // LOADS

        def load(j):
            rows = pl.ds(j * part, part)
            return pltpu.make_async_copy(spectra.at[rows], raw.at[rows], sems.at[j])

        for j in range(LOADS):
            load(j).start()
        for j in range(LOADS):
            load(j).wait()

            def widen(i, _):
                rows = pl.ds(pl.multiple_of(j * part + i * 256, 256), 256)
                wide[rows, :] = raw[rows, :].astype(F32)
                return 0

            lax.fori_loop(0, part // 256, widen, 0)

        def sort(b, _):
            for n in range(64):
                row = pl.multiple_of(place[b * 64 + n], 8)
                sorted_[n * UNIT : (n + 1) * UNIT, :] = wide[pl.ds(row, UNIT), :]
            rows = pl.ds(pl.multiple_of(b * 128, 128), 128)
            for e in range(2 * PER):
                ordered[e, rows, :] = sorted_[pl.ds(e, 128, stride=2 * PER), :].astype(BF16)
            return 0

        lax.fori_loop(0, STATIONS // 64, sort, 0)

    first = pl.multiple_of(lax.axis_index("panel") * 128, 128)
    lre, lim = ordered[ch, pl.ds(first, 128), :], ordered[PER + ch, pl.ds(first, 128), :]
    left = jnp.concatenate(
        [jnp.concatenate([lre, lim], axis=1), jnp.concatenate([lim, -lre], axis=1)], axis=0
    )
    for b in range(8):
        rows = pl.ds(b * 256, 256)
        right = jnp.concatenate([ordered[ch, rows, :], ordered[PER + ch, rows, :]], axis=1)
        prod = lax.dot_general(left, right, NT, preferred_element_type=F32) * (1.0 / FRAMES)
        out[0, 0, :, rows] = prod[:128].astype(BF16)
        out[1, 0, :, rows] = prod[128:].astype(BF16)


def correlate(place, spectra):
    return pl.pallas_call(
        correlate_kernel,
        grid=(PER,),
        out_shape=jax.ShapeDtypeStruct((2, PER, 128, INPUTS), BF16),
        in_specs=[pl.BlockSpec(memory_space=pltpu.SMEM), pl.BlockSpec(memory_space=pl.ANY)],
        out_specs=pl.BlockSpec((2, 1, 128, INPUTS), lambda i: (0, i, 0, 0)),
        scratch_shapes=[
            pltpu.VMEM((PANELS * BLOCK, 128), BF16),
            pltpu.VMEM((PANELS * BLOCK, 128), F32),
            pltpu.VMEM((64 * UNIT, 128), F32),
            pltpu.VMEM((2 * PER, INPUTS, 128), BF16),
            pltpu.SemaphoreType.DMA((LOADS,)),
        ],
        compiler_params=pltpu.CompilerParams(vmem_limit_bytes=56 * 2**20),
        cost_estimate=pl.CostEstimate(flops=2 * 6 * 256 * 2048 * 256, bytes_accessed=13 * 2**20, transcendentals=0),
        name="correlate",
    )(place, spectra)


def local(voltages, prototype, complex_gains, flagged, station_order):
    c = lax.axis_index("chan")
    keep = jnp.repeat(1.0 - flagged.astype(F32), 2)
    gains = (complex_gains * keep[:, None]).T.reshape(GROUPS, PER, 2, LOCAL)
    gains = jnp.pad(gains, ((0, 0), (0, 8 - PER), (0, 0), (0, 0)))
    gre, gim = gains[:, :, 0].reshape(GROUPS * 8, LOCAL), gains[:, :, 1].reshape(GROUPS * 8, LOCAL)
    dev = station_order // (LOCAL // 2)
    cs, ps = dev // PANELS, dev % PANELS
    r = ((cs // 2 - c // 2 + 4) % 4) * 2 + (cs % 2 + c % 2) % 2
    place = ((ps * 8 + r) * (LOCAL // 2) + station_order % (LOCAL // 2)) * UNIT
    pieces = channelize(voltages, prototype, gre, gim)
    spectra = exchange(pieces)
    return correlate(place, spectra)


def solution(mesh):
    placed = (
        P(("chan", "panel"), None),
        P(),
        P(("chan", "panel"), None),
        P(("chan", "panel")),
        P(),
    )
    return jax.shard_map(
        local, mesh=mesh, in_specs=placed, out_specs=P(None, "chan", "panel", None), check_vma=False
    )
```

time: 217 us -> 88.6 us (0.41)
  Pallas kernels: 0 us -> 84.7 us
  local copies, waits for them, and re-layouts: 76.3 us -> 0.92 us
  waiting for transfers between devices: 58.1 us -> 0 us
  matrix products: 42.3 us -> 0 us
  between operations: 13.6 us -> 0.02 us
  blocking collectives: 12.8 us -> 0 us
  other arithmetic: 13.4 us -> 2.74 us
    pallas_call x0 -> x3, Pallas kernels: none -> 84.7 us  [the longest x1 42.8 us: exchange(): pl.pallas_call(exchange_kernel, out_shape=jax.ShapeDtypeStruct((PANELS *...]
    all_gather x1 -> x0, waiting for transfers between devices: 58.1 us -> none  [local(): gathered = lax.all_gather(turned, 'panel', axis=1, tiled=True)]
    dot_general x2 -> x0, matrix products: 42.3 us -> none  [the longest x1 37.8 us: spectra_of(): jnp.einsum('nk,ifn->kif', dft_table, frames_win, preferred_element_type=j...]
    gather x3 -> x0, local copies, waits for them, and re-layouts: 31.9 us -> none  [the longest x1 19.2 us: local(): columns = jnp.take(gathered, local_row, axis=1)]
    reshape x1 -> x0, local copies, waits for them, and re-layouts: 21.9 us -> none  [local(): voltages.reshape(local_inputs, frame_total + tap_count - 1, length)]
    all_to_all x1 -> x0, blocking collectives: 12.8 us -> none  [local(): lax.all_to_all(spectra, 'chan', split_axis=0, concat_axis=1, tiled=True)]
    convert_element_type x2 -> x0, local copies, waits for them, and re-layouts: 8.92 us -> none  [the longest x1 8.63 us: local(): return (accumulated * (1.0 / frame_total)).astype(jnp.bfloat16)]
    select_n x5 -> x0, other arithmetic: 8.9 us -> none  [the longest x2 8.68 us: local(): columns = jnp.take(gathered, local_row, axis=1)]
  transfers between devices with their start and end apart: 1 -> 0, of which waited for: 1 -> 0; matrix products, arithmetic and copies ran while one was open for 4% -> 0% of each run, Pallas kernels for 0% -> 0%
where the time goes in v1:
time: 88.6 us; the launch traced here: 88.4 us
  Pallas kernels  84.7 us (96%)
  other arithmetic  2.74 us (3%)
  local copies, waits for them, and re-layouts  0.92 us (1%)
    pallas_call x1, Pallas kernels, exchange(): pl.pallas_call(exchange_kernel, out_shape=jax.ShapeDtypeStruct((PANELS *...  42.8 us
    pallas_call x1, Pallas kernels, channelize(): pl.pallas_call(channelize_kernel, out_shape=jax.ShapeDtypeStruct((BLOCK,...  31.6 us
    pallas_call x1, Pallas kernels, correlate(): pl.pallas_call(correlate_kernel, grid=(PER,), out_shape=jax.ShapeDtypeStr...  10.3 us

profile of v1, /device:TPU:1, one launch (start us, length us, event | category | flops | bytes accessed | tf_op | source)
XLA Modules:
  0.0 88.4 jit_solution(18201203041855239837)
XLA Ops:
  0.0 0.7 convert_subtract_fusion
  0.7 1.3 %fusion.4.place = s32[1024]{0:T(1024)} fusion(s32[1024]{0:T(1024)} %param.10, s32[]{:T(128)S(6)} %select_n.51, s32[]{:T(128)S(6)} %select_n.48), kind=kLoop, calls=%fused_computation.28 | loop fusion | flops 91136 | bytes 8200 | tf_op jit(solution)/shard_map/mul | solution.py:358
  2.0 0.1 broadcast_in_dim.3
  2.0 0.1 mul.31
  2.1 0.8 multiply_bitcast_fusion
  2.9 0.1 copy.10
  3.0 0.7 pad_slice_fusion
  3.7 31.6 %channelize.1.src = bf16[1536,128]{1,0:T(8,128)(2,1)} custom-call(bf16[16,536576]{1,0:T(8,128)(2,1)} %volt.1, f32[4,4096]{1,0:T(4,128)} %proto.1, bf16[128,4096]{1,0:T(8,128)(2,1)} %constant.113.clone.table, f32[64,16]{1,0:T(8,128)} %bitcast.7, f32[64,16]{1,0:T(8,128)} %bitcast.6), custom_call_target="tpu_custom_call" | custom-call | flops 8791261184 | bytes 20971520 | tf_op jit(solution)/shard_map/channelize/pallas_call | solution.py:100
  35.3 42.8 %exchange.1.spectra = bf16[24576,128]{1,0:T(8,128)(2,1)} custom-call(bf16[1536,128]{1,0:T(8,128)(2,1)} %channelize.1.src), custom_call_target="tpu_custom_call" | custom-call | tf_op jit(solution)/shard_map/exchange/pallas_call | solution.py:263
  78.1 10.3 %correlate.1 = bf16[2,6,128,2048]{3,2,1,0:T(8,128)(2,1)} custom-call(s32[1024]{0:T(1024)} %fusion.4.place, bf16[24576,128]{1,0:T(8,128)(2,1)} %exchange.1.spectra), custom_call_target="tpu_custom_call" | custom-call | flops 1610612736 | bytes 13631488 | tf_op jit(solution)/shard_map/correlate/pallas_call | solution.py:330

commit v2 on v1

v2 whole, which is shorter than its diff:
```python
import functools
import math

import jax
import jax.numpy as jnp
import numpy as np
from jax import lax
from jax.experimental import pallas as pl
from jax.experimental.pallas import tpu as pltpu
from jax.sharding import PartitionSpec as P

MESH = pl.DeviceIdType.MESH
F32, BF16 = jnp.float32, jnp.bfloat16
NT = (((1,), (1,)), ((), ()))

NFFT, TAPS, FRAMES, NCHAN = 4096, 4, 128, 48
INPUTS, STATIONS = 2048, 1024
LOCAL = 16
GROUPS, PER = 8, 6
FALL = FRAMES + TAPS - 1
HALF_IN = LOCAL // 2
PIECE = HALF_IN * 2 * PER
HALF_ROWS = GROUPS * PIECE
BLOCK = 2 * HALF_ROWS
PANELS = 16


def table_rows():
    n = np.arange(NFFT)[None, :]
    j = np.arange(NCHAN)[:, None]
    m = (n * (NFFT // 4 + j)) % NFFT
    phase = m.astype(np.float32) * np.float32(2.0 * math.pi / NFFT)
    both = np.stack([np.cos(phase), -np.sin(phase)], axis=1)
    both = both.reshape(GROUPS, PER, 2, NFFT).transpose(0, 2, 1, 3)
    both = np.pad(both, ((0, 0), (0, 0), (0, 8 - PER), (0, 0)))
    return both.reshape(128, NFFT).astype(jnp.bfloat16)


STEP_F = 34
STARTS = (0, 34, 66, 97)
VOLT_COPIES = 8

CHUNK = BLOCK // 4
HALF = CHUNK // 2
Z_FIRST = (0, 1)
EVENTS = (
    ("own", 0, 0),
    ("own", 0, 1),
    ("near_up", 0, 0),
    ("near_down", 0, 0),
    ("over0", 1, 0),
    ("near_up", 0, 1),
    ("near_down", 0, 1),
    ("over0", 1, 1),
    ("own", 0, 2),
    ("far_up", 0, 0),
    ("far_down", 0, 0),
    ("partner", 1, 2),
    ("over3", 1, 0),
    ("own", 0, 3),
    ("partner", 1, 3),
    ("far_up", 0, 1),
    ("far_down", 0, 1),
    ("over1", 1, 0),
    ("near_up", 0, 2),
    ("near_down", 0, 2),
    ("over3", 1, 1),
    ("near_up", 1, 2),
    ("near_down", 1, 2),
    ("over1", 1, 1),
    ("near_up", 0, 3),
    ("near_down", 0, 3),
    ("over2a", 1, 0),
    ("over2b", 1, 0),
    ("near_up", 1, 3),
    ("near_down", 1, 3),
    ("over2a", 1, 1),
    ("far_up", 0, 2),
    ("far_down", 0, 2),
    ("over2b", 1, 1),
    ("far_up", 1, 2),
    ("far_down", 1, 2),
    ("far_up", 0, 3),
    ("far_down", 0, 3),
    ("far_up", 1, 3),
    ("far_down", 1, 3),
)


def spectra_kernel(
    volt, proto, table, gains, flagged, order, out, place,
    buf, w, y, s, half0, half1, gt, gre, gim, vs, ss, rs, own_sem,
):
    c, p = lax.axis_index("chan"), lax.axis_index("panel")
    x, yl = c // 2, c % 2
    z, h, k = p // 4, (p // 2) % 2, p % 2

    def panel(dz, dh, dk=0):
        return ((z + dz) % 4) * 4 + ((h + dh) % 2) * 2 + (k + dk) % 2

    def at_panel(pan):
        return {"chan": c, "panel": pan}

    def chan_target(r):
        return ((x + 4 - r // 2) % 4) * 2 + (yl + r % 2) % 2

    up, down, over, sib = (at_panel(a) for a in (panel(1, 0), panel(3, 0), panel(0, 1), panel(0, 0, 1)))

    per = -(-FALL // VOLT_COPIES)
    cuts = [(a, min(per, FALL - a)) for a in range(0, FALL, per)]

    def load(i):
        cols = pl.ds(cuts[i][0] * NFFT, cuts[i][1] * NFFT)
        return pltpu.make_async_copy(volt.at[:, cols], buf.at[:, cols], vs.at[i])

    for i in range(len(cuts)):
        load(i).start()

    barrier = pltpu.get_barrier_semaphore()
    greet = [{"chan": chan_target(r), "panel": q} for r in range(1, GROUPS) for q in (p, panel(0, 1))]
    greet += [up, down, over, sib]
    for d in greet:
        pl.semaphore_signal(barrier, inc=1, device_id=d, device_id_type=MESH)

    tab = 512

    def weights(i, _):
        cols = pl.ds(pl.multiple_of(i * tab, tab), tab)
        t = table[:, cols].astype(F32)
        for tap in range(TAPS):
            w[pl.ds(tap * 128, 128), cols] = (t * proto[tap : tap + 1, cols]).astype(BF16)
        return 0

    lax.fori_loop(0, NFFT // tab, weights, 0)

    gt[...] = jnp.zeros_like(gt)
    gt[:LOCAL, : 2 * NCHAN] = gains[...]
    gt[...] = gt[...].T
    gre[...] = jnp.zeros_like(gre)
    gim[...] = jnp.zeros_like(gim)
    for g in range(GROUPS):
        gre[g * 8 : g * 8 + PER, :] = gt[pl.ds(g * 2 * PER, PER, stride=2), :]
        gim[g * 8 : g * 8 + PER, :] = gt[pl.ds(g * 2 * PER + 1, PER, stride=2), :]

    st = order[...]
    dev, within = st // HALF_IN, st % HALF_IN
    cs, ps = dev // PANELS, dev % PANELS
    r = ((cs // 2 - x + 4) % 4) * 2 + (cs % 2 + yl) % 2
    place[...] = ((ps * 2 + within // 4) * GROUPS + r) * PIECE + (within % 4) * (4 * PER)

    waited = [0]

    def channelize(hh, dest):
        low = hh * HALF_IN
        for first in STARTS:
            while waited[0] < len(cuts) and cuts[waited[0]][0] < first + STEP_F:
                load(waited[0]).wait()
                waited[0] += 1
            v = jnp.concatenate(
                [buf[low : low + HALF_IN, pl.ds((first + f) * NFFT, NFFT)] for f in range(STEP_F)], axis=0
            )
            rows = pl.ds(first * HALF_IN, STEP_F * HALF_IN)
            for j in range(2):
                prod = lax.dot_general(v, w[pl.ds(j * 256, 256), :], NT, preferred_element_type=F32)
                y[2 * j, rows, :] = prod[:, :128]
                y[2 * j + 1, rows, :] = prod[:, 128:]
        for i in range(HALF_IN):
            raw = y[0, pl.ds(i, FRAMES, stride=HALF_IN), :]
            for t in range(1, TAPS):
                raw = raw + y[t, pl.ds(t * HALF_IN + i, FRAMES, stride=HALF_IN), :]
            turned = raw.T
            n = low + i
            keep = (1 - flagged[n // 2]).astype(F32)
            for g in range(GROUPS):
                re, im = turned[g * 16 : g * 16 + 8], turned[g * 16 + 8 : g * 16 + 16]
                a, b = gre[g * 8 : g * 8 + 8, n : n + 1] * keep, gim[g * 8 : g * 8 + 8, n : n + 1] * keep
                at = g * PIECE + i * 2 * PER
                s[at : at + PER, :] = (a * re - b * im)[:PER]
                s[at + PER : at + 2 * PER, :] = (a * im + b * re)[:PER]
        dest[...] = s[...].astype(BF16)

    ids, sends = {}, []

    def number(name):
        return ids.setdefault(name, len(ids))

    def region(block, row, rows):
        return out.at[pl.ds(pl.multiple_of(block * BLOCK + row, 16), rows)]

    def send(name, block, row, rows, device, source=None):
        n = number(name)
        there = region(block, row, rows)
        copy = pltpu.make_async_remote_copy(
            there if source is None else source, there, ss.at[n], rs.at[n], device_id=device, device_id_type=MESH
        )
        copy.start()
        sends.append(copy)

    def arrived(name, block, row, rows):
        n = number(name)
        here = region(block, row, rows)
        pltpu.make_async_remote_copy(here, here, ss.at[n], rs.at[n], device_id=sib, device_id_type=MESH).wait_recv()

    mine = panel(0, 0)

    def turn(hh, src):
        row = hh * HALF_ROWS
        pltpu.make_async_copy(
            src.at[pl.ds(pl.multiple_of(c * PIECE, 16), PIECE)], region(mine, row, PIECE), own_sem.at[hh]
        ).start()
        for r in (0, 1, 2, 3, 6, 7, 4, 5):
            t = chan_target(r)
            piece = src.at[pl.ds(pl.multiple_of(t * PIECE, 16), PIECE)]
            if r:
                send(("a", hh, r), mine, row + r * PIECE, PIECE, {"chan": t, "panel": p}, piece)
            if hh * 2 + r // 4 not in Z_FIRST:
                send(("b", hh, r), mine, row + r * PIECE, PIECE, {"chan": t, "panel": panel(0, 1)}, piece)

    shared = []

    def share(place_of, row, rows):
        name = ("s", place_of, row)
        send(name, panel(*place_of), row, rows, sib)
        shared.append((name, place_of, row, rows))

    def pass_on(what, dh, q):
        row, hh = q * CHUNK, q // 2
        z_first = q in Z_FIRST
        if what in ("own", "partner"):
            block = panel(0, dh)
            for r in range(4 * (q % 2), 4 * (q % 2) + 4):
                at = hh * HALF_ROWS + r * PIECE
                if what == "own" and r == 0:
                    here = region(block, at, PIECE)
                    pltpu.make_async_copy(here, here, own_sem.at[hh]).wait()
                else:
                    arrived(("a" if what == "own" else "b", hh, r), block, at, PIECE)
            send(("up", dh, q), block, row, CHUNK, up)
            send(("down", dh, q), block, row, CHUNK, down)
            if z_first:
                send(("y", 0, q), block, row, CHUNK, over)
            share((0, dh), row, CHUNK)
        elif what in ("near_up", "near_down"):
            dz, way, half = (3, up, 0) if what == "near_up" else (1, down, HALF)
            block = panel(dz, dh)
            arrived((what[5:], dh, q), block, row, CHUNK)
            send(("far_" + what[5:], dh, q), block, row + half, HALF, way)
            if z_first:
                send(("y", dz, q), block, row, CHUNK, over)
            share((dz, dh), row, CHUNK)
        elif what in ("far_up", "far_down"):
            at = row + (0 if what == "far_up" else HALF)
            arrived((what, dh, q), panel(2, dh), at, HALF)
            if z_first:
                send(("y2", at), panel(2, dh), at, HALF, over)
            share((2, dh), at, HALF)
        elif what in ("over2a", "over2b"):
            at = row + (0 if what == "over2a" else HALF)
            arrived(("y2", at), panel(2, 1), at, HALF)
            share((2, 1), at, HALF)
        else:
            dz = int(what[4])
            arrived(("y", dz, q), panel(dz, 1), row, CHUNK)
            share((dz, 1), row, CHUNK)

    channelize(0, half0)
    pl.semaphore_wait(barrier, len(greet))
    turn(0, half0)
    channelize(1, half1)
    turn(1, half1)
    for event in EVENTS:
        pass_on(*event)
    for name, (dz, dh), row, rows in shared:
        arrived(name, panel(dz, dh, 1), row, rows)
    for copy in sends:
        copy.wait_send()


def spectra_of_all(volt, proto, gains, flagged, order):
    vm, sm = pl.BlockSpec(memory_space=pltpu.VMEM), pl.BlockSpec(memory_space=pltpu.SMEM)
    anywhere = pl.BlockSpec(memory_space=pl.ANY)
    many = 160
    return pl.pallas_call(
        spectra_kernel,
        out_shape=(
            jax.ShapeDtypeStruct((PANELS * BLOCK, 128), BF16),
            jax.ShapeDtypeStruct((8, 128), jnp.int32),
        ),
        in_specs=[anywhere, vm, vm, vm, sm, vm],
        out_specs=(anywhere, vm),
        scratch_shapes=[
            pltpu.VMEM((LOCAL, FALL * NFFT), BF16),
            pltpu.VMEM((TAPS * 128, NFFT), BF16),
            pltpu.VMEM((TAPS, FALL * HALF_IN, 128), F32),
            pltpu.VMEM((HALF_ROWS, 128), F32),
            pltpu.VMEM((HALF_ROWS, 128), BF16),
            pltpu.VMEM((HALF_ROWS, 128), BF16),
            pltpu.VMEM((128, 128), F32),
            pltpu.VMEM((GROUPS * 8, 128), F32),
            pltpu.VMEM((GROUPS * 8, 128), F32),
            pltpu.SemaphoreType.DMA((VOLT_COPIES,)),
            pltpu.SemaphoreType.DMA((many,)),
            pltpu.SemaphoreType.DMA((many,)),
            pltpu.SemaphoreType.DMA((2,)),
        ],
        compiler_params=pltpu.CompilerParams(
            collective_id=0, has_side_effects=True, vmem_limit_bytes=56 * 2**20
        ),
        name="spectra",
    )(volt, proto, jnp.asarray(table_rows()), gains, flagged, order)


LOADS = 8
UNIT = 2 * 2 * PER


def correlate_kernel(place, spectra, out, raw, wide, sorted_, ordered, sems):
    ch = pl.program_id(0)

    @pl.when(ch == 0)
    def _():
        part = PANELS * BLOCK // LOADS

        def load(j):
            rows = pl.ds(j * part, part)
            return pltpu.make_async_copy(spectra.at[rows], raw.at[rows], sems.at[j])

        for j in range(LOADS):
            load(j).start()
        for j in range(LOADS):
            load(j).wait()

            def widen(i, _):
                rows = pl.ds(pl.multiple_of(j * part + i * 256, 256), 256)
                wide[rows, :] = raw[rows, :].astype(F32)
                return 0

            lax.fori_loop(0, part // 256, widen, 0)

        def sort(b, _):
            for n in range(64):
                row = pl.multiple_of(place[b // 2, (b % 2) * 64 + n], 8)
                sorted_[n * UNIT : (n + 1) * UNIT, :] = wide[pl.ds(row, UNIT), :]
            rows = pl.ds(pl.multiple_of(b * 128, 128), 128)
            for e in range(2 * PER):
                ordered[e, rows, :] = sorted_[pl.ds(e, 128, stride=2 * PER), :].astype(BF16)
            return 0

        lax.fori_loop(0, STATIONS // 64, sort, 0)

    first = pl.multiple_of(lax.axis_index("panel") * 128, 128)
    lre, lim = ordered[ch, pl.ds(first, 128), :], ordered[PER + ch, pl.ds(first, 128), :]
    left = jnp.concatenate(
        [jnp.concatenate([lre, lim], axis=1), jnp.concatenate([lim, -lre], axis=1)], axis=0
    )
    for b in range(8):
        rows = pl.ds(b * 256, 256)
        right = jnp.concatenate([ordered[ch, rows, :], ordered[PER + ch, rows, :]], axis=1)
        prod = lax.dot_general(left, right, NT, preferred_element_type=F32) * (1.0 / FRAMES)
        out[0, 0, :, rows] = prod[:128].astype(BF16)
        out[1, 0, :, rows] = prod[128:].astype(BF16)


def correlate(place, spectra):
    return pl.pallas_call(
        correlate_kernel,
        grid=(PER,),
        out_shape=jax.ShapeDtypeStruct((2, PER, 128, INPUTS), BF16),
        in_specs=[pl.BlockSpec(memory_space=pltpu.SMEM), pl.BlockSpec(memory_space=pl.ANY)],
        out_specs=pl.BlockSpec((2, 1, 128, INPUTS), lambda i: (0, i, 0, 0)),
        scratch_shapes=[
            pltpu.VMEM((PANELS * BLOCK, 128), BF16),
            pltpu.VMEM((PANELS * BLOCK, 128), F32),
            pltpu.VMEM((64 * UNIT, 128), F32),
            pltpu.VMEM((2 * PER, INPUTS, 128), BF16),
            pltpu.SemaphoreType.DMA((LOADS,)),
        ],
        compiler_params=pltpu.CompilerParams(vmem_limit_bytes=56 * 2**20),
        cost_estimate=pl.CostEstimate(flops=2 * 6 * 256 * 2048 * 256, bytes_accessed=13 * 2**20, transcendentals=0),
        name="correlate",
    )(place, spectra)


def local(voltages, prototype, complex_gains, flagged, station_order):
    spectra, place = spectra_of_all(
        voltages, prototype, complex_gains, flagged, station_order.reshape(8, 128)
    )
    return correlate(place, spectra)


def solution(mesh):
    placed = (
        P(("chan", "panel"), None),
        P(),
        P(("chan", "panel"), None),
        P(("chan", "panel")),
        P(),
    )
    return jax.shard_map(
        local, mesh=mesh, in_specs=placed, out_specs=P(None, "chan", "panel", None), check_vma=False
    )
```

time: 88.6 us -> 66.5 us (0.75)
  the two profiles are of different devices: /device:TPU:1 before, /device:TPU:21 now
where the time goes in v2:
time: 66.5 us; the launch traced here: 66.3 us
  Pallas kernels  66.3 us (100%)
    pallas_call x1, Pallas kernels, spectra_of_all(): pl.pallas_call(spectra_kernel, out_shape=(jax.ShapeDtypeStruct((PANELS *...  54.6 us
    pallas_call x1, Pallas kernels, correlate(): pl.pallas_call(correlate_kernel, grid=(PER,), out_shape=jax.ShapeDtypeStr...  11.7 us

profile of v2, /device:TPU:21, one launch (start us, length us, event | category | flops | bytes accessed | tf_op | source)
XLA Modules:
  0.0 66.3 jit_solution(6926325369089192072)
XLA Ops:
  0.0 54.6 %spectra.1 = (bf16[24576,128]{1,0:T(8,128)(2,1)}, s32[8,128]{1,0:T(8,128)}) custom-call(bf16[16,536576]{1,0:T(8,128)(2,1)} %volt.1, f32[4,4096]{1,0:T(4,128)} %proto.1, bf16[128,4096]{1,0:T(8,128)(2,1)} %constant.2.clone.table, f32[16,96]{1,0:T(8,128)} %gains.1, s32[8]{0:T(128)} %flagged.1, s32[8,128]{1,0:T(8,128)} %bitcast.1), custom_call_target="tpu_custom_call" | custom-call | tf_op jit(solution)/shard_map/spectra/pallas_call | solution.py:283
  54.6 11.7 %correlate.1 = bf16[2,6,128,2048]{3,2,1,0:T(8,128)(2,1)} custom-call(s32[8,128]{1,0:T(8,128)} %get-tuple-element.7.place, bf16[24576,128]{1,0:T(8,128)(2,1)} %get-tuple-element.8.spectra), custom_call_target="tpu_custom_call" | custom-call | flops 1610612736 | bytes 13631488 | tf_op jit(solution)/shard_map/correlate/pallas_call | solution.py:365

commit v3 on v2

--- a/solution.py
+++ b/solution.py
@@ -36,6 +36,7 @@
     return both.reshape(128, NFFT).astype(jnp.bfloat16)
 
 
+RECEIVES = 41
 STEP_F = 34
 STARTS = (0, 34, 66, 97)
 VOLT_COPIES = 8
@@ -191,15 +192,15 @@
         n = number(name)
         there = region(block, row, rows)
         copy = pltpu.make_async_remote_copy(
-            there if source is None else source, there, ss.at[n], rs.at[n], device_id=device, device_id_type=MESH
+            there if source is None else source, there, ss, rs.at[n], device_id=device, device_id_type=MESH
         )
         copy.start()
-        sends.append(copy)
+        sends.append(rows)
 
     def arrived(name, block, row, rows):
         n = number(name)
         here = region(block, row, rows)
-        pltpu.make_async_remote_copy(here, here, ss.at[n], rs.at[n], device_id=sib, device_id_type=MESH).wait_recv()
+        pltpu.make_async_remote_copy(here, here, ss, rs.at[n], device_id=sib, device_id_type=MESH).wait_recv()
 
     mine = panel(0, 0)
 
@@ -212,29 +213,27 @@
             t = chan_target(r)
             piece = src.at[pl.ds(pl.multiple_of(t * PIECE, 16), PIECE)]
             if r:
-                send(("a", hh, r), mine, row + r * PIECE, PIECE, {"chan": t, "panel": p}, piece)
+                send(("a", hh * 2 + r // 4), mine, row + r * PIECE, PIECE, {"chan": t, "panel": p}, piece)
             if hh * 2 + r // 4 not in Z_FIRST:
-                send(("b", hh, r), mine, row + r * PIECE, PIECE, {"chan": t, "panel": panel(0, 1)}, piece)
+                send(("b", hh * 2 + r // 4), mine, row + r * PIECE, PIECE, {"chan": t, "panel": panel(0, 1)}, piece)
 
     shared = []
 
     def share(place_of, row, rows):
-        name = ("s", place_of, row)
-        send(name, panel(*place_of), row, rows, sib)
-        shared.append((name, place_of, row, rows))
+        send("share", panel(*place_of), row, rows, sib)
+        shared.append(rows)
 
     def pass_on(what, dh, q):
         row, hh = q * CHUNK, q // 2
         z_first = q in Z_FIRST
         if what in ("own", "partner"):
             block = panel(0, dh)
-            for r in range(4 * (q % 2), 4 * (q % 2) + 4):
-                at = hh * HALF_ROWS + r * PIECE
-                if what == "own" and r == 0:
-                    here = region(block, at, PIECE)
-                    pltpu.make_async_copy(here, here, own_sem.at[hh]).wait()
-                else:
-                    arrived(("a" if what == "own" else "b", hh, r), block, at, PIECE)
+            skip = 0
+            if what == "own" and q % 2 == 0:
+                skip = PIECE
+                here = region(block, row, PIECE)
+                pltpu.make_async_copy(here, here, own_sem.at[hh]).wait()
+            arrived(("a" if what == "own" else "b", q), block, row + skip, CHUNK - skip)
             send(("up", dh, q), block, row, CHUNK, up)
             send(("down", dh, q), block, row, CHUNK, down)
             if z_first:
@@ -270,16 +269,14 @@
     turn(1, half1)
     for event in EVENTS:
         pass_on(*event)
-    for name, (dz, dh), row, rows in shared:
-        arrived(name, panel(dz, dh, 1), row, rows)
-    for copy in sends:
-        copy.wait_send()
+    arrived("share", 0, 0, sum(shared))
+    gone = out.at[pl.ds(0, sum(sends))]
+    pltpu.make_async_remote_copy(gone, gone, ss, rs.at[0], device_id=sib, device_id_type=MESH).wait_send()
 
 
 def spectra_of_all(volt, proto, gains, flagged, order):
     vm, sm = pl.BlockSpec(memory_space=pltpu.VMEM), pl.BlockSpec(memory_space=pltpu.SMEM)
     anywhere = pl.BlockSpec(memory_space=pl.ANY)
-    many = 160
     return pl.pallas_call(
         spectra_kernel,
         out_shape=(
@@ -299,8 +296,8 @@
             pltpu.VMEM((GROUPS * 8, 128), F32),
             pltpu.VMEM((GROUPS * 8, 128), F32),
             pltpu.SemaphoreType.DMA((VOLT_COPIES,)),
-            pltpu.SemaphoreType.DMA((many,)),
-            pltpu.SemaphoreType.DMA((many,)),
+            pltpu.SemaphoreType.DMA,
+            pltpu.SemaphoreType.DMA((RECEIVES,)),
             pltpu.SemaphoreType.DMA((2,)),
         ],
         compiler_params=pltpu.CompilerParams(
@@ -314,66 +311,79 @@
 UNIT = 2 * 2 * PER
 
 
-def correlate_kernel(place, spectra, out, raw, wide, sorted_, ordered, sems):
-    ch = pl.program_id(0)
-
-    @pl.when(ch == 0)
-    def _():
-        part = PANELS * BLOCK // LOADS
-
-        def load(j):
-            rows = pl.ds(j * part, part)
-            return pltpu.make_async_copy(spectra.at[rows], raw.at[rows], sems.at[j])
-
-        for j in range(LOADS):
-            load(j).start()
-        for j in range(LOADS):
-            load(j).wait()
-
-            def widen(i, _):
-                rows = pl.ds(pl.multiple_of(j * part + i * 256, 256), 256)
-                wide[rows, :] = raw[rows, :].astype(F32)
-                return 0
-
-            lax.fori_loop(0, part // 256, widen, 0)
-
-        def sort(b, _):
-            for n in range(64):
-                row = pl.multiple_of(place[b // 2, (b % 2) * 64 + n], 8)
-                sorted_[n * UNIT : (n + 1) * UNIT, :] = wide[pl.ds(row, UNIT), :]
-            rows = pl.ds(pl.multiple_of(b * 128, 128), 128)
-            for e in range(2 * PER):
-                ordered[e, rows, :] = sorted_[pl.ds(e, 128, stride=2 * PER), :].astype(BF16)
+WIDTH = 256
+COLUMNS = INPUTS // WIDTH
+
+
+def correlate_kernel(place, spectra, out, raw, wide, sorted_, left, result, sems, out_sems):
+    part = PANELS * BLOCK // LOADS
+
+    def load(j):
+        rows = pl.ds(j * part, part)
+        return pltpu.make_async_copy(spectra.at[rows], raw.at[rows], sems.at[j])
+
+    for j in range(LOADS):
+        load(j).start()
+    for j in range(LOADS):
+        load(j).wait()
+
+        def widen(i, _):
+            rows = pl.ds(pl.multiple_of(j * part + i * 256, 256), 256)
+            wide[rows, :] = raw[rows, :].astype(F32)
             return 0
 
-        lax.fori_loop(0, STATIONS // 64, sort, 0)
-
-    first = pl.multiple_of(lax.axis_index("panel") * 128, 128)
-    lre, lim = ordered[ch, pl.ds(first, 128), :], ordered[PER + ch, pl.ds(first, 128), :]
-    left = jnp.concatenate(
-        [jnp.concatenate([lre, lim], axis=1), jnp.concatenate([lim, -lre], axis=1)], axis=0
-    )
-    for b in range(8):
-        rows = pl.ds(b * 256, 256)
-        right = jnp.concatenate([ordered[ch, rows, :], ordered[PER + ch, rows, :]], axis=1)
-        prod = lax.dot_general(left, right, NT, preferred_element_type=F32) * (1.0 / FRAMES)
-        out[0, 0, :, rows] = prod[:128].astype(BF16)
-        out[1, 0, :, rows] = prod[128:].astype(BF16)
+        lax.fori_loop(0, part // 256, widen, 0)
+
+    def sort(line, first, stations):
+        for n in range(stations):
+            row = pl.multiple_of(place[line, first + n], 8)
+            sorted_[n * UNIT : (n + 1) * UNIT, :] = wide[pl.ds(row, UNIT), :]
+
+    def part_of(e, rows):
+        return sorted_[pl.ds(e, rows, stride=2 * PER), :].astype(BF16)
+
+    p = lax.axis_index("panel")
+    sort(p // 2, (p % 2) * 64, 64)
+    for ch in range(PER):
+        re, im = part_of(ch, 128), part_of(PER + ch, 128)
+        left[ch, :128, :128] = re
+        left[ch, :128, 128:] = im
+        left[ch, 128:, :128] = im
+        left[ch, 128:, 128:] = -re
+
+    def write(b):
+        columns = pl.ds(pl.multiple_of(b * WIDTH, WIDTH), WIDTH)
+        return pltpu.make_async_copy(result.at[b], out.at[:, :, :, columns], out_sems.at[b])
+
+    def block(b, _):
+        sort(b, 0, WIDTH // 2)
+        for ch in range(PER):
+            right = jnp.concatenate([part_of(ch, WIDTH), part_of(PER + ch, WIDTH)], axis=1)
+            prod = lax.dot_general(left[ch], right, NT, preferred_element_type=F32) * (1.0 / FRAMES)
+            result[b, 0, ch] = prod[:128].astype(BF16)
+            result[b, 1, ch] = prod[128:].astype(BF16)
+        write(b).start()
+        return 0
+
+    lax.fori_loop(0, COLUMNS, block, 0)
+    for b in range(COLUMNS):
+        write(b).wait()
 
 
 def correlate(place, spectra):
     return pl.pallas_call(
         correlate_kernel,
-        grid=(PER,),
         out_shape=jax.ShapeDtypeStruct((2, PER, 128, INPUTS), BF16),
         in_specs=[pl.BlockSpec(memory_space=pltpu.SMEM), pl.BlockSpec(memory_space=pl.ANY)],
-        out_specs=pl.BlockSpec((2, 1, 128, INPUTS), lambda i: (0, i, 0, 0)),
+        out_specs=pl.BlockSpec(memory_space=pl.ANY),
         scratch_shapes=[
             pltpu.VMEM((PANELS * BLOCK, 128), BF16),
             pltpu.VMEM((PANELS * BLOCK, 128), F32),
-            pltpu.VMEM((64 * UNIT, 128), F32),
-            pltpu.VMEM((2 * PER, INPUTS, 128), BF16),
+            pltpu.VMEM((WIDTH // 2 * UNIT, 128), F32),
+            pltpu.VMEM((PER, 256, 256), BF16),
+            pltpu.VMEM((COLUMNS, 2, PER, 128, WIDTH), BF16),
             pltpu.SemaphoreType.DMA((LOADS,)),
+            pltpu.SemaphoreType.DMA((COLUMNS,)),
         ],
         compiler_params=pltpu.CompilerParams(vmem_limit_bytes=56 * 2**20),
         cost_estimate=pl.CostEstimate(flops=2 * 6 * 256 * 2048 * 256, bytes_accessed=13 * 2**20, transcendentals=0),

time: 66.5 us -> 61.3 us (0.922)
  Pallas kernels: 66.3 us -> 61.1 us
    pallas_call x1, Pallas kernels: 54.6 us -> 52 us  [spectra_of_all(): pl.pallas_call(spectra_kernel, out_shape=(jax.ShapeDtypeStruct((PANELS *...]
    pallas_call x1, Pallas kernels: 11.7 us -> 9.14 us  [correlate(): pl.pallas_call(correlate_kernel, out_shape=jax.ShapeDtypeStruct((2, PER,...]
where the time goes in v3:
time: 61.3 us; the launch traced here: 61.1 us
  Pallas kernels  61.1 us (100%)
    pallas_call x1, Pallas kernels, spectra_of_all(): pl.pallas_call(spectra_kernel, out_shape=(jax.ShapeDtypeStruct((PANELS *...  52 us
    pallas_call x1, Pallas kernels, correlate(): pl.pallas_call(correlate_kernel, out_shape=jax.ShapeDtypeStruct((2, PER,...  9.14 us

profile of v3, /device:TPU:21, one launch (start us, length us, event | category | flops | bytes accessed | tf_op | source)
XLA Modules:
  0.0 61.1 jit_solution(7952332300852906578)
XLA Ops:
  0.0 52.0 %spectra.1 = (bf16[24576,128]{1,0:T(8,128)(2,1)}, s32[8,128]{1,0:T(8,128)}) custom-call(bf16[16,536576]{1,0:T(8,128)(2,1)} %volt.1, f32[4,4096]{1,0:T(4,128)} %proto.1, bf16[128,4096]{1,0:T(8,128)(2,1)} %constant.2.clone.table, f32[16,96]{1,0:T(8,128)} %gains.1, s32[8]{0:T(128)} %flagged.1, s32[8,128]{1,0:T(8,128)} %bitcast.1), custom_call_target="tpu_custom_call" | custom-call | tf_op jit(solution)/shard_map/spectra/pallas_call | solution.py:280
  52.0 9.1 %correlate.1 = bf16[2,6,128,2048]{3,2,1,0:T(8,128)(2,1)} custom-call(s32[8,128]{1,0:T(8,128)} %get-tuple-element.7.place, bf16[24576,128]{1,0:T(8,128)(2,1)} %get-tuple-element.8.spectra), custom_call_target="tpu_custom_call" | custom-call | flops 1610612736 | bytes 13631488 | tf_op jit(solution)/shard_map/correlate/pallas_call | solution.py:374

commit v4 on v3

--- a/solution.py
+++ b/solution.py
@@ -41,50 +41,52 @@
 STARTS = (0, 34, 66, 97)
 VOLT_COPIES = 8
 
-CHUNK = BLOCK // 4
+PER_HALF = 2
+AT_ONCE = GROUPS // PER_HALF
+CHUNK = HALF_ROWS // PER_HALF
 HALF = CHUNK // 2
-Z_FIRST = (0, 1)
+Z_FIRST = (0, 2)
 EVENTS = (
     ("own", 0, 0),
     ("own", 0, 1),
+    ("partner", 1, 1),
     ("near_up", 0, 0),
     ("near_down", 0, 0),
     ("over0", 1, 0),
     ("near_up", 0, 1),
     ("near_down", 0, 1),
-    ("over0", 1, 1),
     ("own", 0, 2),
+    ("over3", 1, 0),
+    ("near_up", 1, 1),
+    ("near_down", 1, 1),
+    ("own", 0, 3),
+    ("partner", 1, 3),
     ("far_up", 0, 0),
     ("far_down", 0, 0),
-    ("partner", 1, 2),
-    ("over3", 1, 0),
-    ("own", 0, 3),
-    ("partner", 1, 3),
+    ("over1", 1, 0),
     ("far_up", 0, 1),
     ("far_down", 0, 1),
-    ("over1", 1, 0),
+    ("over0", 1, 2),
     ("near_up", 0, 2),
     ("near_down", 0, 2),
-    ("over3", 1, 1),
-    ("near_up", 1, 2),
-    ("near_down", 1, 2),
-    ("over1", 1, 1),
+    ("over2a", 1, 0),
+    ("far_up", 1, 1),
+    ("far_down", 1, 1),
+    ("over2b", 1, 0),
     ("near_up", 0, 3),
     ("near_down", 0, 3),
-    ("over2a", 1, 0),
-    ("over2b", 1, 0),
+    ("over3", 1, 2),
     ("near_up", 1, 3),
     ("near_down", 1, 3),
-    ("over2a", 1, 1),
+    ("over1", 1, 2),
     ("far_up", 0, 2),
     ("far_down", 0, 2),
-    ("over2b", 1, 1),
-    ("far_up", 1, 2),
-    ("far_down", 1, 2),
     ("far_up", 0, 3),
     ("far_down", 0, 3),
     ("far_up", 1, 3),
     ("far_down", 1, 3),
+    ("over2a", 1, 2),
+    ("over2b", 1, 2),
 )
 
 
@@ -151,7 +153,7 @@
 
     waited = [0]
 
-    def channelize(hh, dest):
+    def channelize(hh, dest, between=None):
         low = hh * HALF_IN
         for first in STARTS:
             while waited[0] < len(cuts) and cuts[waited[0]][0] < first + STEP_F:
@@ -165,6 +167,8 @@
                 prod = lax.dot_general(v, w[pl.ds(j * 256, 256), :], NT, preferred_element_type=F32)
                 y[2 * j, rows, :] = prod[:, :128]
                 y[2 * j + 1, rows, :] = prod[:, 128:]
+        if between is not None:
+            between()
         for i in range(HALF_IN):
             raw = y[0, pl.ds(i, FRAMES, stride=HALF_IN), :]
             for t in range(1, TAPS):
@@ -213,9 +217,9 @@
             t = chan_target(r)
             piece = src.at[pl.ds(pl.multiple_of(t * PIECE, 16), PIECE)]
             if r:
-                send(("a", hh * 2 + r // 4), mine, row + r * PIECE, PIECE, {"chan": t, "panel": p}, piece)
-            if hh * 2 + r // 4 not in Z_FIRST:
-                send(("b", hh * 2 + r // 4), mine, row + r * PIECE, PIECE, {"chan": t, "panel": panel(0, 1)}, piece)
+                send(("a", hh * PER_HALF + r // AT_ONCE), mine, row + r * PIECE, PIECE, {"chan": t, "panel": p}, piece)
+            if hh * PER_HALF + r // AT_ONCE not in Z_FIRST:
+                send(("b", hh * PER_HALF + r // AT_ONCE), mine, row + r * PIECE, PIECE, {"chan": t, "panel": panel(0, 1)}, piece)
 
     shared = []
 
@@ -224,12 +228,12 @@
         shared.append(rows)
 
     def pass_on(what, dh, q):
-        row, hh = q * CHUNK, q // 2
+        row, hh = q * CHUNK, q // PER_HALF
         z_first = q in Z_FIRST
         if what in ("own", "partner"):
             block = panel(0, dh)
             skip = 0
-            if what == "own" and q % 2 == 0:
+            if what == "own" and q % PER_HALF == 0:
                 skip = PIECE
                 here = region(block, row, PIECE)
                 pltpu.make_async_copy(here, here, own_sem.at[hh]).wait()
@@ -265,9 +269,17 @@
     channelize(0, half0)
     pl.semaphore_wait(barrier, len(greet))
     turn(0, half0)
-    channelize(1, half1)
+    first = tuple(e for e in EVENTS if e[0] == "own" and e[2] < PER_HALF)
+
+    def pass_first():
+        for event in first:
+            pass_on(*event)
+
+    channelize(1, half1, pass_first)
     turn(1, half1)
     for event in EVENTS:
+        if event in first:
+            continue
         pass_on(*event)
     arrived("share", 0, 0, sum(shared))
     gone = out.at[pl.ds(0, sum(sends))]

time: 61.3 us -> 56.4 us (0.920)
  the two profiles are of different devices: /device:TPU:21 before, /device:TPU:1 now
where the time goes in v4:
time: 56.4 us; the launch traced here: 56.2 us
  Pallas kernels  56.2 us (100%)
    pallas_call x1, Pallas kernels, spectra_of_all(): pl.pallas_call(spectra_kernel, out_shape=(jax.ShapeDtypeStruct((PANELS *...  47.1 us
    pallas_call x1, Pallas kernels, correlate(): pl.pallas_call(correlate_kernel, out_shape=jax.ShapeDtypeStruct((2, PER,...  9.13 us

profile of v4, /device:TPU:1, one launch (start us, length us, event | category | flops | bytes accessed | tf_op | source)
XLA Modules:
  0.0 56.2 jit_solution(18020458023774926301)
XLA Ops:
  0.0 47.1 %spectra.1 = (bf16[24576,128]{1,0:T(8,128)(2,1)}, s32[8,128]{1,0:T(8,128)}) custom-call(bf16[16,536576]{1,0:T(8,128)(2,1)} %volt.1, f32[4,4096]{1,0:T(4,128)} %proto.1, bf16[128,4096]{1,0:T(8,128)(2,1)} %constant.2.clone.table, f32[16,96]{1,0:T(8,128)} %gains.1, s32[8]{0:T(128)} %flagged.1, s32[8,128]{1,0:T(8,128)} %bitcast.1), custom_call_target="tpu_custom_call" | custom-call | tf_op jit(solution)/shard_map/spectra/pallas_call | solution.py:292
  47.1 9.1 %correlate.1 = bf16[2,6,128,2048]{3,2,1,0:T(8,128)(2,1)} custom-call(s32[8,128]{1,0:T(8,128)} %get-tuple-element.7.place, bf16[24576,128]{1,0:T(8,128)(2,1)} %get-tuple-element.8.spectra), custom_call_target="tpu_custom_call" | custom-call | flops 1610612736 | bytes 13631488 | tf_op jit(solution)/shard_map/correlate/pallas_call | solution.py:386

commit v5 on v4

--- a/solution.py
+++ b/solution.py
@@ -346,18 +346,18 @@
 
         lax.fori_loop(0, part // 256, widen, 0)
 
-    def sort(line, first, stations):
+    def sort(line, first, stations, slot):
         for n in range(stations):
             row = pl.multiple_of(place[line, first + n], 8)
-            sorted_[n * UNIT : (n + 1) * UNIT, :] = wide[pl.ds(row, UNIT), :]
-
-    def part_of(e, rows):
-        return sorted_[pl.ds(e, rows, stride=2 * PER), :].astype(BF16)
+            sorted_[slot, n * UNIT : (n + 1) * UNIT, :] = wide[pl.ds(row, UNIT), :]
+
+    def part_of(e, rows, slot):
+        return sorted_[slot, pl.ds(e, rows, stride=2 * PER), :].astype(BF16)
 
     p = lax.axis_index("panel")
-    sort(p // 2, (p % 2) * 64, 64)
+    sort(p // 2, (p % 2) * 64, 64, 0)
     for ch in range(PER):
-        re, im = part_of(ch, 128), part_of(PER + ch, 128)
+        re, im = part_of(ch, 128, 0), part_of(PER + ch, 128, 0)
         left[ch, :128, :128] = re
         left[ch, :128, 128:] = im
         left[ch, 128:, :128] = im
@@ -367,17 +367,24 @@
         columns = pl.ds(pl.multiple_of(b * WIDTH, WIDTH), WIDTH)
         return pltpu.make_async_copy(result.at[b], out.at[:, :, :, columns], out_sems.at[b])
 
-    def block(b, _):
-        sort(b, 0, WIDTH // 2)
+    def multiply(b, slot):
         for ch in range(PER):
-            right = jnp.concatenate([part_of(ch, WIDTH), part_of(PER + ch, WIDTH)], axis=1)
+            right = jnp.concatenate([part_of(ch, WIDTH, slot), part_of(PER + ch, WIDTH, slot)], axis=1)
             prod = lax.dot_general(left[ch], right, NT, preferred_element_type=F32) * (1.0 / FRAMES)
             result[b, 0, ch] = prod[:128].astype(BF16)
             result[b, 1, ch] = prod[128:].astype(BF16)
         write(b).start()
+
+    def blocks(pair, _):
+        b = 2 * pair
+        sort(b + 1, 0, WIDTH // 2, 1)
+        multiply(b, 0)
+        sort(jnp.minimum(b + 2, COLUMNS - 1), 0, WIDTH // 2, 0)
+        multiply(b + 1, 1)
         return 0
 
-    lax.fori_loop(0, COLUMNS, block, 0)
+    sort(0, 0, WIDTH // 2, 0)
+    lax.fori_loop(0, COLUMNS // 2, blocks, 0)
     for b in range(COLUMNS):
         write(b).wait()
 
@@ -391,7 +398,7 @@
         scratch_shapes=[
             pltpu.VMEM((PANELS * BLOCK, 128), BF16),
             pltpu.VMEM((PANELS * BLOCK, 128), F32),
-            pltpu.VMEM((WIDTH // 2 * UNIT, 128), F32),
+            pltpu.VMEM((2, WIDTH // 2 * UNIT, 128), F32),
             pltpu.VMEM((PER, 256, 256), BF16),
             pltpu.VMEM((COLUMNS, 2, PER, 128, WIDTH), BF16),
             pltpu.SemaphoreType.DMA((LOADS,)),

time: 56.4 us -> 55.6 us (0.986)
  Pallas kernels: 56.2 us -> 55.5 us
    pallas_call x1, Pallas kernels: 9.13 us -> 8.38 us  [correlate(): pl.pallas_call(correlate_kernel, out_shape=jax.ShapeDtypeStruct((2, PER,...]
where the time goes in v5:
time: 55.6 us; the launch traced here: 55.5 us
  Pallas kernels  55.5 us (100%)
    pallas_call x1, Pallas kernels, spectra_of_all(): pl.pallas_call(spectra_kernel, out_shape=(jax.ShapeDtypeStruct((PANELS *...  47.1 us
    pallas_call x1, Pallas kernels, correlate(): pl.pallas_call(correlate_kernel, out_shape=jax.ShapeDtypeStruct((2, PER,...  8.38 us

profile of v5, /device:TPU:1, one launch (start us, length us, event | category | flops | bytes accessed | tf_op | source)
XLA Modules:
  0.0 55.5 jit_solution(10902862191749819711)
XLA Ops:
  0.0 47.1 %spectra.1 = (bf16[24576,128]{1,0:T(8,128)(2,1)}, s32[8,128]{1,0:T(8,128)}) custom-call(bf16[16,536576]{1,0:T(8,128)(2,1)} %volt.1, f32[4,4096]{1,0:T(4,128)} %proto.1, bf16[128,4096]{1,0:T(8,128)(2,1)} %constant.2.clone.table, f32[16,96]{1,0:T(8,128)} %gains.1, s32[8]{0:T(128)} %flagged.1, s32[8,128]{1,0:T(8,128)} %bitcast.1), custom_call_target="tpu_custom_call" | custom-call | tf_op jit(solution)/shard_map/spectra/pallas_call | solution.py:292
  47.1 8.4 %correlate.1 = bf16[2,6,128,2048]{3,2,1,0:T(8,128)(2,1)} custom-call(s32[8,128]{1,0:T(8,128)} %get-tuple-element.7.place, bf16[24576,128]{1,0:T(8,128)(2,1)} %get-tuple-element.8.spectra), custom_call_target="tpu_custom_call" | custom-call | flops 1610612736 | bytes 13631488 | tf_op jit(solution)/shard_map/correlate/pallas_call | solution.py:393
